TPU v7x, 32 devices: a whole 2x2x4 slice. The times are simulated.
32 devices in a mesh: groups: 2 (over y), chan: 4 (over z), space: 2 (over x), pair: 2 (over core).
Axes of the slice: x: 2, y: 2, z: 4, core: 2. Of those that a mesh axis runs over, the one named last changes fastest.
Arguments:
- grad_out: bfloat16 [512, 32, 1024], P('chan', ('groups', 'space', 'pair')), parts along dimension 1, may hold values from -6 to 6
- conv_weight: bfloat16 [27, 512, 512], P(None, 'chan'), may hold values from -0.0546875 to 0.0546875
- pre_act: bfloat16 [32, 1024, 512], P(('groups', 'space', 'pair'), 'chan'), parts along dimension 0, may hold values from -6 to 6
- down_weight: bfloat16 [8, 256, 512], replicated, may hold values from -0.25 to 0.25
Outputs:
- grad_fine: bfloat16 [32, 1024, 8, 256], P(('groups', 'space', 'pair'), 'chan'), parts along dimension 0
There are 2 independent parts, one for each index of `groups`. A program takes and returns all parts, laid end to end along the dimension named above; an argument that names none is the same for every part. Nothing has to cross between parts.
All inputs are finite; a program needn't handle non-finite values.
Results may differ from a plain program's by a relative error of at most 0.025.
Values may be sent and summed in bfloat16 or wider, within the bound.
A program may use at most 64 MiB of HBM per device.

v0:
```python
import math

import jax
import jax.numpy as jnp
from jax import lax
from jax.sharding import PartitionSpec as P

NZ = 8


def with_halo(cells, sides, width):
    for axis, dim in sides:
        count = lax.axis_size(axis)
        ends = count - 1
        head = lax.slice_in_dim(cells, 0, width, axis=dim)
        tail = lax.slice_in_dim(cells, cells.shape[dim] - width, cells.shape[dim], axis=dim)
        cells = jnp.concatenate(
            [
                lax.ppermute(tail, axis, [(i, (i + 1) % count) for i in range(ends)]),
                cells,
                lax.ppermute(head, axis, [((i + 1) % count, i) for i in range(ends)]),
            ],
            axis=dim,
        )
    return cells


def shifted_stack(padded, depth):
    extent = padded.shape[1] - 2
    plane_len = padded.shape[2]
    widened = jnp.pad(padded, ((0, 0), (0, 0), (depth + 1, depth + 1)))
    z_index = jnp.arange(plane_len, dtype=jnp.int32) % depth
    pieces = []
    for step_x in (-1, 0, 1):
        x_rows = widened[:, 1 - step_x : 1 - step_x + extent, :]
        for step_y in (-1, 0, 1):
            for step_z in (-1, 0, 1):
                offset = step_y * depth + step_z
                piece = x_rows[:, :, depth + 1 - offset : depth + 1 - offset + plane_len]
                inside = (z_index - step_z >= 0) & (z_index - step_z < depth)
                pieces.append(jnp.where(inside, piece, jnp.zeros_like(piece)))
    return jnp.stack(pieces)


def gelu_slope(values):
    return 0.5 * (1.0 + jax.scipy.special.erf(values / math.sqrt(2.0))) + values * jnp.exp(
        -0.5 * values * values
    ) / math.sqrt(2.0 * math.pi)


def body(grad_out, conv_weight, pre_act, down_weight):
    padded = with_halo(grad_out, ((("space", "pair"), 1),), 1)
    stacked = shifted_stack(padded, NZ)
    partial_sum = lax.dot_general(
        stacked, conv_weight, (((0, 1), (0, 1)), ((), ())), preferred_element_type=jnp.float32
    )
    owned = lax.psum_scatter(
        partial_sum.astype(jnp.bfloat16), "chan", scatter_dimension=2, tiled=True
    )
    grad_act = lax.all_to_all(owned, "chan", split_axis=1, concat_axis=2, tiled=True)
    values = pre_act.astype(jnp.float32)
    grad_pre = (grad_act.astype(jnp.float32) * gelu_slope(values)).astype(jnp.bfloat16)
    result = lax.dot_general(
        grad_pre, down_weight, (((2,), (2,)), ((), ())), preferred_element_type=jnp.float32
    )
    return result.astype(jnp.bfloat16)


def solution(mesh):
    in_specs = (
        P("chan", ("groups", "space", "pair"), None),
        P(None, "chan", None),
        P(("groups", "space", "pair"), "chan", None),
        P(),
    )
    out_specs = P(("groups", "space", "pair"), "chan", None, None)
    return jax.shard_map(body, mesh=mesh, in_specs=in_specs, out_specs=out_specs, check_vma=False)
```

profile of v0, /device:TPU:0, one launch (start us, length us, event | category | flops | bytes accessed | tf_op | source)
XLA Modules:
  0.0 204.0 jit_solution(13061538225299000226)
XLA Ops:
  6.5 2.8 %copy.39 = bf16[128,4,1024]{0,2,1:T(8,128)(2,1)} copy(bf16[128,4,1024]{2,1,0:T(4,128)(2,1)} %param.4) | data formatting | bytes 2097152 | tf_op args[0]
  9.3 1.2 fusion.98
  10.5 2.4 %collective-permute-start = (bf16[128,1,1024]{0,2,1:T(8,128)(2,1)S(1)}, bf16[128,1,1024]{0,2,1:T(8,128)(2,1)S(1)}, u32[]{:S(2)}, u32[]{:S(2)}) collective-permute-start(bf16[128,1,1024]{0,2,1:T(8,128)(2,1)S(1)} %get-tuple-element.5), channel_id=1, source_target_pairs={{0,1},{1,2},{2,3},{4,5},{5,6},{6,7},{8,9},{9,10},{10,11},{12,13},{... | collective-permute-start | bytes 786440 | tf_op jit(solution)/shard_map/ppermute | solution.py:19
  12.9 1.3 collective-permute-start.1
  14.2 4.2 %collective-permute-done.1 = bf16[128,1,1024]{0,2,1:T(8,128)(2,1)S(1)} collective-permute-done((bf16[128,1,1024]{0,2,1:T(8,128)(2,1)S(1)}, bf16[128,1,1024]{0,2,1:T(8,128)(2,1)S(1)}, u32[]{:S(2)}, u32[]{:S(2)}) %collective-permute-start.1) | collective-permute-done | bytes 262176 | tf_op jit(solution)/shard_map/ppermute | solution.py:21
  18.4 1.6 fusion.18
  23.1 0.6 fusion.59
  23.7 0.6 fusion.57
  24.8 0.6 fusion.53
  25.4 0.6 fusion.51
  29.8 0.6 fusion.37
  30.4 0.6 fusion.35
  33.1 0.8 fusion.24
  35.0 17.0 %bitcast_convert_fusion = bf16[4,1024,512]{2,1,0:T(8,128)(2,1)} fusion(bf16[27,128,4,1024]{1,3,0,2:T(8,128)(2,1)S(1)} %fusion.20, bf16[27,128,512]{2,1,0:T(8,128)(2,1)S(1)} %copy-done), kind=kOutput, calls=%fused_computation | convolution fusion | flops 14497611776 | bytes 36044800 | tf_op jit(solution)/shard_map/dot_general | solution.py:54
  52.0 8.0 %copy.76 = bf16[4,1024,512]{1,0,2:T(4,128)(2,1)} copy(bf16[4,1024,512]{2,1,0:T(8,128)(2,1)} %bitcast_convert_fusion) | data formatting | bytes 8388608
  60.0 6.5 %copy.79 = bf16[64,8,4,1024]{3,1,2,0:T(8,128)(2,1)} copy(bf16[64,8,4,1024]{3,2,1,0:T(4,128)(2,1)} %bitcast.184) | data formatting | bytes 8388608
  66.5 81.7 %reduce-scatter.4.cloned.1.call-done = bf16[128,4096]{1,0:T(8,128)(2,1)} async-done(((bf16[512,4096]{1,0:T(8,128)(2,1)}), bf16[128,4096]{1,0:T(8,128)(2,1)}) %reduce-scatter.4.cloned.1.call-update) | async-done | bytes 1048592
  148.2 1.8 reshape.11
  150.0 1.5 copy.71
  151.5 29.8 %all_to_all.4 = bf16[4,1024,128]{2,0,1:T(4,128)(2,1)S(1)} all-to-all(bf16[4,1024,128]{2,0,1:T(4,128)(2,1)S(1)} %copy.71), channel_id=1, replica_groups=mesh['groups'=2,'chan'=4,'space'=2,'pair'=2] {'chan'}, dimensions={1} | all-to-all | bytes 2097152 | tf_op jit(solution)/shard_map/all_to_all | solution.py:60
  181.4 2.7 %copy.72 = f32[4,256,4,128]{3,2,1,0:T(4,128)} copy(f32[4,256,4,128]{3,0,1,2:T(4,128)S(1)} %convert_bitcast_fusion) | data formatting | bytes 4194304 | tf_op jit(solution)/shard_map/convert_element_type | solution.py:62
  184.1 3.3 %reshape.4 = f32[4,256,512]{2,1,0:T(8,128)} reshape(f32[4,256,4,128]{3,2,1,0:T(4,128)} %copy.72) | data formatting | bytes 4194304 | tf_op jit(solution)/shard_map/convert_element_type | solution.py:62
  187.4 5.3 %convolution_convert_fusion = bf16[4,256,8,256]{3,1,2,0:T(8,128)(2,1)S(1)} fusion(bf16[8,256,512]{2,1,0:T(8,128)(2,1)} %param.7, f32[4,256,512]{2,1,0:T(8,128)} %reshape.4, bf16[4,256,512]{2,1,0:T(8,128)(2,1)} %param.6), kind=kOutput, calls=%fused_computation.10 | convolution fusion | flops 2155347968 | bytes 9437184 | tf_op jit(solution)/shard_map/dot_general | solution.py:63
  192.7 4.5 %copy.73 = bf16[4,256,8,256]{3,2,1,0:T(8,128)(2,1)} copy(bf16[4,256,8,256]{3,1,2,0:T(8,128)(2,1)S(1)} %convolution_convert_fusion) | data formatting | bytes 8388608 | tf_op jit(solution)/shard_map/convert_element_type | solution.py:66
  (33 shorter events, 10.5 us)
Async XLA Ops:
  6.5 28.4 %copy-start = (bf16[27,128,512]{2,1,0:T(8,128)(2,1)S(1)}, bf16[27,128,512]{2,1,0:T(8,128)(2,1)}, u32[]{:S(2)}) copy-start(bf16[27,128,512]{2,1,0:T(8,128)(2,1)} %param.5) | copy-start | bytes 10616836
  6.5 141.6 %reduce-scatter.4.cloned.1.call-start = ((), (), s32[]{:S(2)}) async-start(), calls=%async_computation.2 | async-start | bytes 5242880
  9.3 12.8 %copy-start.2 = (bf16[128,4,1024]{0,2,1:T(8,128)(2,1)S(1)}, bf16[128,4,1024]{0,2,1:T(8,128)(2,1)}, u32[]{:S(2)}) copy-start(bf16[128,4,1024]{0,2,1:T(8,128)(2,1)} %copy.39) | copy-start | bytes 3145732
  10.5 3.7 %collective-permute-start = (bf16[128,1,1024]{0,2,1:T(8,128)(2,1)S(1)}, bf16[128,1,1024]{0,2,1:T(8,128)(2,1)S(1)}, u32[]{:S(2)}, u32[]{:S(2)}) collective-permute-start(bf16[128,1,1024]{0,2,1:T(8,128)(2,1)S(1)} %get-tuple-element.5), channel_id=1, source_target_pairs={{0,1},{1,2},{2,3},{4,5},{5,6},{6,7},{8,9},{9,10},{10,11},{12,13},{... | collective-permute-start | bytes 786440 | tf_op jit(solution)/shard_map/ppermute | solution.py:19
  12.9 5.5 %collective-permute-start.1 = (bf16[128,1,1024]{0,2,1:T(8,128)(2,1)S(1)}, bf16[128,1,1024]{0,2,1:T(8,128)(2,1)S(1)}, u32[]{:S(2)}, u32[]{:S(2)}) collective-permute-start(bf16[128,1,1024]{0,2,1:T(8,128)(2,1)S(1)} %get-tuple-element.6), channel_id=1, source_target_pairs={{1,0},{2,1},{3,2},{5,4},{6,5},{7,6},{9,8},{10,9},{11,10},{13,12},{... | collective-permute-start | bytes 786440 | tf_op jit(solution)/shard_map/ppermute | solution.py:21
  184.1 13.1 %copy-start.1 = (bf16[27,128,512]{2,1,0:T(8,128)(2,1)S(1)}, bf16[27,128,512]{2,1,0:T(8,128)(2,1)}, u32[]{:S(2)}) copy-start(bf16[27,128,512]{2,1,0:T(8,128)(2,1)} %param.5) | copy-start | bytes 10616836
Sparse Core Ops, SparseCore 0:
  66.6 81.4 reduce-scatter.3
where the time goes:
time: 204 us
  waiting for transfers between devices  85.8 us (42%)
  local copies, waits for them, and re-layouts  32.2 us (16%)
  blocking collectives  29.8 us (15%)
  matrix products  22.4 us (11%)
  other arithmetic  16.5 us (8%)
  between operations  13.7 us (7%)
  starting transfers between devices  3.67 us (2%)
    unnamed x2, waiting for transfers between devices  81.7 us
    all_to_all x1, blocking collectives, body(): lax.all_to_all(owned, 'chan', split_axis=1, concat_axis=2, tiled=True)  29.8 us
    unnamed x10, local copies, waits for them, and re-layouts  19.1 us
    dot_general x1, matrix products, body(): lax.dot_general(stacked, conv_weight, (((0, 1), (0, 1)), ((), ())), prefe...  17 us
    unnamed x26, other arithmetic  14.2 us
    convert_element_type x2, local copies, waits for them, and re-layouts, body(): grad_act.astype(jnp.float32) * gelu_slope(values)  5.93 us
    dot_general x1, matrix products, body(): lax.dot_general(grad_pre, down_weight, (((2,), (2,)), ((), ())), preferre...  5.33 us
    convert_element_type x1, local copies, waits for them, and re-layouts, body(): return result.astype(jnp.bfloat16)  4.47 us
  transfers between devices with their start and end apart: 3, of which 2 were waited for; matrix products, arithmetic and copies ran while one was open for 0% of the time, Pallas kernels for 0%

commit v1 on v0

--- a/solution.py
+++ b/solution.py
@@ -1,11 +1,15 @@
+import functools
 import math
 
 import jax
 import jax.numpy as jnp
 from jax import lax
+from jax.experimental import pallas as pl
+from jax.experimental.pallas import tpu as pltpu
 from jax.sharding import PartitionSpec as P
 
 NZ = 8
+MESH = pl.DeviceIdType.MESH
 
 
 def with_halo(cells, sides, width):
@@ -48,22 +52,347 @@
     ) / math.sqrt(2.0 * math.pi)
 
 
-def body(grad_out, conv_weight, pre_act, down_weight):
-    padded = with_halo(grad_out, ((("space", "pair"), 1),), 1)
-    stacked = shifted_stack(padded, NZ)
-    partial_sum = lax.dot_general(
-        stacked, conv_weight, (((0, 1), (0, 1)), ((), ())), preferred_element_type=jnp.float32
-    )
-    owned = lax.psum_scatter(
-        partial_sum.astype(jnp.bfloat16), "chan", scatter_dimension=2, tiled=True
-    )
-    grad_act = lax.all_to_all(owned, "chan", split_axis=1, concat_axis=2, tiled=True)
+def finish(grad_act, pre_act, down_weight):
     values = pre_act.astype(jnp.float32)
     grad_pre = (grad_act.astype(jnp.float32) * gelu_slope(values)).astype(jnp.bfloat16)
     result = lax.dot_general(
         grad_pre, down_weight, (((2,), (2,)), ((), ())), preferred_element_type=jnp.float32
     )
     return result.astype(jnp.bfloat16)
+
+
+def body_blocks(grad_out, conv_weight, pre_act, down_weight):
+    padded = with_halo(grad_out, ((("space", "pair"), 1),), 1)
+    stacked = shifted_stack(padded, NZ)
+    partial_sum = lax.dot_general(
+        stacked, conv_weight, (((0, 1), (0, 1)), ((), ())), preferred_element_type=jnp.float32
+    )
+    grad_act = lax.psum_scatter(
+        partial_sum.astype(jnp.bfloat16), "chan", scatter_dimension=1, tiled=True
+    )
+    return finish(grad_act, pre_act, down_weight)
+
+
+def conv_kernel(
+    n, ns, nx, ny, s_ref, w_ref, out_ref,
+    w_all, cells, shifted, acc,
+    w_send, w_recv, g_send, g_recv, h_send, h_recv, local,
+):
+    gy, z = lax.axis_index("groups"), lax.axis_index("chan")
+    sx, core = lax.axis_index("space"), lax.axis_index("pair")
+    main = NZ * ny
+    taps, rows, piece_rows = 27, w_all.shape[1], w_all.shape[1] // 8
+    to_x = {"space": sx + 1 - 2 * lax.rem(sx, 2)}
+    to_y = {"groups": 1 - gy}
+    to_core = {"pair": 1 - core}
+    cross_space = sx + 2 * core - 1
+    to_cross = {"space": cross_space, "pair": 1 - core}
+    has_cross = (cross_space >= 0) & (cross_space < ns)
+    q = gy * 4 + lax.rem(sx, 2) * 2 + core
+
+    def flip(index, gy_flip, x_flip, core_flip):
+        g = 1 - gy if gy_flip else gy
+        x = 1 - lax.rem(sx, 2) if x_flip else lax.rem(sx, 2)
+        c = 1 - core if core_flip else core
+        return g * 4 + x * 2 + c
+
+    q_x, q_y, q_d = flip(q, 0, 1, 0), flip(q, 1, 0, 0), flip(q, 1, 1, 0)
+    pieces = (q, q_x, q_y, q_d)
+    partner_pieces = (flip(q, 0, 0, 1), flip(q, 0, 1, 1), flip(q, 1, 0, 1), flip(q, 1, 1, 1))
+
+    barrier = pltpu.get_barrier_semaphore()
+    for hop in range(1, n):
+        pl.semaphore_signal(
+            barrier, inc=1, device_id={"chan": lax.rem(z + hop, n)}, device_id_type=MESH
+        )
+    for target in (to_x, to_y, to_core):
+        pl.semaphore_signal(barrier, inc=1, device_id=target, device_id_type=MESH)
+
+    @pl.when(has_cross)
+    def _():
+        pl.semaphore_signal(barrier, inc=1, device_id=to_cross, device_id_type=MESH)
+
+    own_w = pltpu.make_async_copy(w_ref, w_all.at[z], local.at[0])
+    own_g = pltpu.make_async_copy(s_ref.at[z], cells.at[z, pl.ds(1, nx)], local.at[1])
+    own_w.start()
+    own_g.start()
+
+    @pl.when(has_cross)
+    def _():
+        pl.semaphore_wait(barrier, n + 3)
+
+    @pl.when(jnp.logical_not(has_cross))
+    def _():
+        pl.semaphore_wait(barrier, n + 2)
+
+    def w_rows(piece):
+        return pl.ds(pl.multiple_of(piece * piece_rows, piece_rows), piece_rows)
+
+    def w_copy(kind, way, step, shard, piece, target):
+        view = w_all.at[shard, w_rows(piece)]
+        return pltpu.make_async_remote_copy(
+            src_ref=view, dst_ref=view,
+            send_sem=w_send.at[kind, way, step], recv_sem=w_recv.at[kind, way, step],
+            device_id=target, device_id_type=MESH,
+        )
+
+    def own_z_copy(way):
+        return pltpu.make_async_remote_copy(
+            src_ref=w_ref.at[w_rows(q)], dst_ref=w_all.at[z, w_rows(q)],
+            send_sem=w_send.at[0, way, 1], recv_sem=w_recv.at[0, way, 1],
+            device_id={"chan": z + 1 - 2 * way}, device_id_type=MESH,
+        )
+
+    def g_copy(way, step):
+        target = z + step * (1 - 2 * way)
+        return pltpu.make_async_remote_copy(
+            src_ref=s_ref.at[target], dst_ref=cells.at[z, pl.ds(1, nx)],
+            send_sem=g_send.at[way, step], recv_sem=g_recv.at[way, step],
+            device_id={"chan": target}, device_id_type=MESH,
+        )
+
+    def g_arrival(way, step):
+        shard = z - step * (1 - 2 * way)
+        return pltpu.make_async_remote_copy(
+            src_ref=s_ref.at[z], dst_ref=cells.at[shard, pl.ds(1, nx)],
+            send_sem=g_send.at[way, step], recv_sem=g_recv.at[way, step],
+            device_id={"chan": shard}, device_id_type=MESH,
+        )
+
+    def h_copy(side, way, step, shard, sending):
+        last = nx + 1
+        if side == 0:
+            source, landing, target = nx - (nx - 1) * core, last * core, to_core
+            arriving = last * (1 - core)
+        else:
+            source, landing, target = 1 + (nx - 1) * core, last * (1 - core), to_cross
+            arriving = last * core
+        return pltpu.make_async_remote_copy(
+            src_ref=cells.at[shard, source],
+            dst_ref=cells.at[shard, landing if sending else arriving],
+            send_sem=h_send.at[side, way, step], recv_sem=h_recv.at[side, way, step],
+            device_id=target, device_id_type=MESH,
+        )
+
+    def sends_on(way, step):
+        return z + step < n if way == 0 else z - step >= 0
+
+    def arrives(way, step):
+        return z - step >= 0 if way == 0 else z + step < n
+
+    def shard_of(way, step):
+        return z - step if way == 0 else z + step
+
+    def each_arrival(step, act):
+        for way in (0, 1):
+            @pl.when(arrives(way, step))
+            def _():
+                act(way, step, shard_of(way, step))
+
+    for step in range(1, n):
+        for way in (0, 1):
+            @pl.when(sends_on(way, step))
+            def _():
+                g_copy(way, step).start()
+                if step == 1:
+                    own_z_copy(way).start()
+
+    def start_halo(way, step, shard):
+        h_copy(0, way, step, shard, True).start()
+
+        @pl.when(has_cross)
+        def _():
+            h_copy(1, way, step, shard, True).start()
+
+        @pl.when(jnp.logical_not(has_cross))
+        def _():
+            cells[shard, (nx + 1) * core] = jnp.zeros(cells.shape[2:], cells.dtype)
+
+    def end_halo(way, step, shard):
+        h_copy(0, way, step, shard, False).wait_recv()
+
+        @pl.when(has_cross)
+        def _():
+            h_copy(1, way, step, shard, False).wait_recv()
+
+        def plane(x, carry):
+            values = cells[shard, x, pl.ds(0, main)]
+            edge = cells[shard, x, pl.ds(main, 2 * NZ)].astype(jnp.float32)
+            wide = values.astype(jnp.float32)
+            width = wide.shape[1]
+            row = lax.broadcasted_iota(jnp.int32, (main, width), 0) % ny
+            low = jnp.broadcast_to(edge[:NZ][:, None, :], (NZ, ny, width)).reshape(main, width)
+            high = jnp.broadcast_to(edge[NZ:][:, None, :], (NZ, ny, width)).reshape(main, width)
+            after = jnp.where(row == ny - 1, high, pltpu.roll(wide, main - 1, 0))
+            before = jnp.where(row == 0, low, pltpu.roll(wide, 1, 0))
+            shifted[0, shard, x, pl.ds(ny, main)] = after.astype(jnp.bfloat16)
+            shifted[1, shard, x, pl.ds(ny, main)] = values
+            shifted[2, shard, x, pl.ds(ny, main)] = before.astype(jnp.bfloat16)
+            blank = jnp.zeros((ny, width), jnp.bfloat16)
+            for kind in range(3):
+                shifted[kind, shard, x, pl.ds(0, ny)] = blank
+                shifted[kind, shard, x, pl.ds(ny + main, ny)] = blank
+            return carry
+
+        lax.fori_loop(0, nx + 2, plane, 0)
+
+    def stage_a(way, step, shard):
+        w_copy(0, way, step, shard, q, to_core).wait_recv()
+        w_copy(5, way, step, shard, q, to_x).start()
+        w_copy(6, way, step, shard, q, to_y).start()
+        if step < n - 1:
+            @pl.when(sends_on(way, 1))
+            def _():
+                w_copy(0, way, step + 1, shard, q, {"chan": z + 1 - 2 * way}).start()
+        w_copy(1, way, step, shard, q, to_core).start()
+        g_arrival(way, step).wait_recv()
+        start_halo(way, step, shard)
+
+    def stage_b(way, step, shard):
+        w_copy(5, way, step, shard, q_x, to_x).wait_recv()
+
+        @pl.when(core == 0)
+        def _():
+            w_copy(7, way, step, shard, q_x, to_y).start()
+
+        w_copy(2, way, step, shard, q_x, to_core).start()
+        w_copy(6, way, step, shard, q_y, to_y).wait_recv()
+
+        @pl.when(core == 1)
+        def _():
+            w_copy(7, way, step, shard, q_y, to_x).start()
+
+        w_copy(3, way, step, shard, q_y, to_core).start()
+
+    def stage_c(way, step, shard):
+        w_copy(7, way, step, shard, q_d, to_y).wait_recv()
+        w_copy(4, way, step, shard, q_d, to_core).start()
+
+    def multiply(shard, first):
+        width = cells.shape[3]
+        weights = w_all.at[shard]
+
+        def planes(half, carry):
+            parts = []
+            for step_x in (-1, 0, 1):
+                for step_y in (-1, 0, 1):
+                    for step_z in (-1, 0, 1):
+                        part = shifted[
+                            step_y + 1, shard, pl.ds(half * 2 + 1 - step_x, 2),
+                            pl.ds((1 - step_z) * ny, main),
+                        ]
+                        parts.append(part.reshape(2 * main, width))
+            product = jnp.dot(
+                jnp.concatenate(parts, axis=1), weights[...],
+                preferred_element_type=jnp.float32,
+            ).reshape(2, main, out_ref.shape[2])
+            if first:
+                acc[pl.ds(half * 2, 2)] = product
+            else:
+                acc[pl.ds(half * 2, 2)] += product
+            return carry
+
+        lax.fori_loop(0, nx // 2, planes, 0)
+
+    def compute(way, step, shard):
+        end_halo(way, step, shard)
+        for kind in range(4):
+            w_copy(1 + kind, way, step, shard, partner_pieces[kind], to_core).wait_recv()
+        multiply(shard, False)
+
+    own_g.wait()
+    start_halo(0, 0, z)
+    own_w.wait()
+    end_halo(0, 0, z)
+    each_arrival(1, stage_a)
+    multiply(z, True)
+    for step in range(1, n):
+        each_arrival(step, stage_b)
+        if step + 1 < n:
+            each_arrival(step + 1, stage_a)
+        each_arrival(step, stage_c)
+        each_arrival(step, compute)
+    out_ref[...] = acc[...].astype(out_ref.dtype)
+
+    def end_sends(way, step, shard):
+        w_copy(5, way, step, shard, q, to_x).wait_send()
+        w_copy(6, way, step, shard, q, to_y).wait_send()
+        for kind in range(4):
+            w_copy(1 + kind, way, step, shard, pieces[kind], to_core).wait_send()
+
+        @pl.when(core == 0)
+        def _():
+            w_copy(7, way, step, shard, q_x, to_y).wait_send()
+
+        @pl.when(core == 1)
+        def _():
+            w_copy(7, way, step, shard, q_y, to_x).wait_send()
+
+        if step < n - 1:
+            @pl.when(sends_on(way, 1))
+            def _():
+                w_copy(0, way, step + 1, shard, q, {"chan": z + 1 - 2 * way}).wait_send()
+        end_halo_sends(way, step, shard)
+
+    def end_halo_sends(way, step, shard):
+        h_copy(0, way, step, shard, True).wait_send()
+
+        @pl.when(has_cross)
+        def _():
+            h_copy(1, way, step, shard, True).wait_send()
+
+    end_halo_sends(0, 0, z)
+    for step in range(1, n):
+        each_arrival(step, end_sends)
+        for way in (0, 1):
+            @pl.when(sends_on(way, step))
+            def _():
+                g_copy(way, step).wait_send()
+                if step == 1:
+                    own_z_copy(way).wait_send()
+
+
+def body_gather(n, ns, grad_out, conv_weight, pre_act, down_weight):
+    channels, nx, plane = grad_out.shape
+    rows_y = plane // NZ
+    ny = rows_y // n
+    wide = conv_weight.shape[2]
+    main = NZ * ny
+    turned = grad_out.reshape(channels, nx, rows_y, NZ).transpose(1, 3, 2, 0)
+    edged = jnp.pad(turned, ((0, 0), (0, 0), (1, 1), (0, 0)))
+    blocks = turned.reshape(nx, NZ, n, ny, channels).transpose(2, 0, 1, 3, 4)
+    blocks = blocks.reshape(n, nx, main, channels)
+    low = edged[:, :, 0 : rows_y : ny].transpose(2, 0, 1, 3)
+    high = edged[:, :, ny + 1 :: ny].transpose(2, 0, 1, 3)
+    send = jnp.concatenate([blocks, low, high], axis=2)
+    weights = conv_weight.reshape(-1, wide)
+    vmem = pltpu.VMEM
+    dma = pltpu.SemaphoreType.DMA
+    grad_act = pl.pallas_call(
+        functools.partial(conv_kernel, n, ns, nx, ny),
+        out_shape=jax.ShapeDtypeStruct((nx, main, wide), jnp.bfloat16),
+        in_specs=[pl.BlockSpec(memory_space=pl.ANY)] * 2,
+        out_specs=pl.BlockSpec(memory_space=pltpu.VMEM),
+        scratch_shapes=[
+            vmem((n, weights.shape[0], wide), jnp.bfloat16),
+            vmem((n, nx + 2, main + 2 * NZ, channels), jnp.bfloat16),
+            vmem((3, n, nx + 2, main + 2 * ny, channels), jnp.bfloat16),
+            vmem((nx, main, wide), jnp.float32),
+            dma((8, 2, n)), dma((8, 2, n)),
+            dma((2, n)), dma((2, n)),
+            dma((2, 2, n)), dma((2, 2, n)),
+            dma((2,)),
+        ],
+        compiler_params=pltpu.CompilerParams(
+            collective_id=0, has_side_effects=True, vmem_limit_bytes=56 * 2**20
+        ),
+        cost_estimate=pl.CostEstimate(
+            flops=2 * 27 * n * channels * nx * main * wide,
+            bytes_accessed=8 * 2**20, transcendentals=0,
+        ),
+    )(send, weights)
+    grad_act = grad_act.reshape(nx, NZ, ny, wide).transpose(0, 2, 1, 3).reshape(nx, main, wide)
+    return finish(grad_act, pre_act, down_weight)
 
 
 def solution(mesh):
@@ -74,4 +403,15 @@
         P(),
     )
     out_specs = P(("groups", "space", "pair"), "chan", None, None)
+    n, ns = mesh.shape["chan"], mesh.shape["space"]
+
+    def body(grad_out, conv_weight, pre_act, down_weight):
+        channels, nx, plane = grad_out.shape
+        ny = plane // NZ // n
+        fits = channels % 128 == 0 and ny % 16 == 0 and nx % 2 == 0 and ns % 2 == 0
+        fits = fits and mesh.shape["groups"] == 2 and mesh.shape["pair"] == 2
+        if fits:
+            return body_gather(n, ns, grad_out, conv_weight, pre_act, down_weight)
+        return body_blocks(grad_out, conv_weight, pre_act, down_weight)
+
     return jax.shard_map(body, mesh=mesh, in_specs=in_specs, out_specs=out_specs, check_vma=False)

time: 204 us -> 101 us (0.50)
  waiting for transfers between devices: 85.8 us -> 0 us
  Pallas kernels: 0 us -> 85.7 us
  blocking collectives: 29.8 us -> 0 us
  local copies, waits for them, and re-layouts: 32.2 us -> 6.98 us
  matrix products: 22.4 us -> 3.64 us
  other arithmetic: 16.5 us -> 2.66 us
  between operations: 13.7 us -> 0.08 us
  starting transfers between devices: 3.67 us -> 0 us
    pallas_call x0 -> x1, Pallas kernels: none -> 85.7 us  [body_gather(): pl.pallas_call(functools.partial(conv_kernel, n, ns, nx, ny), out_shape=j...]
    unnamed x2 -> x0, waiting for transfers between devices: 81.7 us -> none
    all_to_all x1 -> x0, blocking collectives: 29.8 us -> none  [body(): lax.all_to_all(owned, 'chan', split_axis=1, concat_axis=2, tiled=True)]
    dot_general x2 -> x1, matrix products: 22.4 us -> 3.64 us  [finish(): lax.dot_general(grad_pre, down_weight, (((2,), (2,)), ((), ())), preferre...]
    unnamed x10 -> x5, local copies, waits for them, and re-layouts: 19.1 us -> 2.08 us
    unnamed x26 -> x0, other arithmetic: 14.2 us -> none
    convert_element_type x3 -> x1, local copies, waits for them, and re-layouts: 10.4 us -> 4.47 us  [finish(): return result.astype(jnp.bfloat16)]
    ppermute x2 -> x0, waiting for transfers between devices: 4.17 us -> none  [the longest x1 4.17 us: with_halo(): lax.ppermute(head, axis, [((i + 1) % count, i) for i in range(ends)])]
  transfers between devices with their start and end apart: 3 -> 0, of which waited for: 2 -> 0; matrix products, arithmetic and copies ran while one was open for 0% -> 0% of each run, Pallas kernels for 0% -> 0%
where the time goes in v1:
time: 101 us; the launch traced here: 99 us
  Pallas kernels  85.7 us (85%)
  local copies, waits for them, and re-layouts  6.98 us (7%)
  matrix products  3.64 us (4%)
  other arithmetic  2.66 us (3%)
    pallas_call x1, Pallas kernels, body_gather(): pl.pallas_call(functools.partial(conv_kernel, n, ns, nx, ny), out_shape=j...  85.7 us
    convert_element_type x1, local copies, waits for them, and re-layouts, finish(): return result.astype(jnp.bfloat16)  4.47 us
    dot_general x1, matrix products, finish(): lax.dot_general(grad_pre, down_weight, (((2,), (2,)), ((), ())), preferre...  3.64 us
    unnamed x5, local copies, waits for them, and re-layouts  2.08 us

profile of v1, /device:TPU:0, one launch (start us, length us, event | category | flops | bytes accessed | tf_op | source)
XLA Modules:
  0.0 99.0 jit_solution(7171031112525768223)
XLA Ops:
  0.0 0.0 copy-start
  0.0 2.1 %copy.8 = bf16[128,4,1024]{0,2,1:T(8,128)(2,1)S(1)} copy(bf16[128,4,1024]{2,1,0:T(4,128)(2,1)} %param.4) | data formatting | bytes 2097152 | tf_op args[0]
  2.1 0.2 copy.10
  2.3 0.2 copy_bitcast_fusion
  2.5 1.1 %pad_maximum_fusion.s_ref = bf16[4,4,272,128]{3,2,1,0:T(8,128)(2,1)} fusion(bf16[4,4,8,128]{3,2,1,0:T(8,128)(2,1)S(1)} %get-tuple-element.6, bf16[4,4,8,128]{3,2,1,0:T(8,128)(2,1)S(1)} %get-tuple-element.5, bf16[4,4,256,128]{3,2,1,0:T(8,128)(2,1)S(1)} %bitcast.35), kind=kLoop, calls=%fused_computation.15 | loop fusion | flops 3342336 | bytes 2228224 | tf_op jit(solution)/shard_map/concatenate | solution.py:367
  3.6 85.7 %shard_map.46 = bf16[4,256,512]{2,1,0:T(8,128)(2,1)} custom-call(bf16[4,4,272,128]{3,2,1,0:T(8,128)(2,1)} %pad_maximum_fusion.s_ref, bf16[3456,512]{1,0:T(8,128)(2,1)} %bitcast.37), custom_call_target="tpu_custom_call" | custom-call | flops 14495514624 | bytes 8388608 | tf_op jit(solution)/shard_map/pallas_call | solution.py:371
  89.3 0.0 copy-start.1
  89.3 1.6 %convert_bitcast_fusion = f32[4,32,8,512]{3,1,2,0:T(8,128)S(1)} fusion(bf16[4,8,32,512]{3,2,1,0:T(8,128)(2,1)} %bitcast.36), kind=kLoop, calls=%fused_computation.12 | loop fusion | flops 524288 | bytes 3145728 | tf_op jit(solution)/shard_map/convert_element_type | solution.py:57
  90.9 0.0 copy-done
  90.9 0.0 copy-done.1
  90.9 3.6 %convolution_convert_fusion = bf16[4,256,8,256]{3,1,2,0:T(8,128)(2,1)S(1)} fusion(bf16[8,256,512]{2,1,0:T(8,128)(2,1)S(1)} %copy-done, bf16[4,256,512]{2,1,0:T(8,128)(2,1)S(1)} %copy-done.1, f32[4,32,8,512]{3,1,2,0:T(8,128)S(1)} %convert_bitcast_fusion), kind=kOutput, calls=%fused_computation.4 | convolution fusion | flops 2155347968 | bytes 9437184 | tf_op jit(solution)/shard_map/dot_general | solution.py:58
  94.6 4.5 %copy.12 = bf16[4,256,8,256]{3,2,1,0:T(8,128)(2,1)} copy(bf16[4,256,8,256]{3,1,2,0:T(8,128)(2,1)S(1)} %convolution_convert_fusion) | data formatting | bytes 8388608 | tf_op jit(solution)/shard_map/convert_element_type | solution.py:61
  (1 shorter events, 0.0 us)
Async XLA Ops:
  0.0 90.9 %copy-start = (bf16[8,256,512]{2,1,0:T(8,128)(2,1)S(1)}, bf16[8,256,512]{2,1,0:T(8,128)(2,1)}, u32[]{:S(2)}) copy-start(bf16[8,256,512]{2,1,0:T(8,128)(2,1)} %param.7) | copy-start | bytes 6291460
  89.3 1.6 %copy-start.1 = (bf16[4,256,512]{2,1,0:T(8,128)(2,1)S(1)}, bf16[4,256,512]{2,1,0:T(8,128)(2,1)}, u32[]{:S(2)}) copy-start(bf16[4,256,512]{2,1,0:T(8,128)(2,1)} %param.6) | copy-start | bytes 3145732

commit v2 on v1

--- a/solution.py
+++ b/solution.py
@@ -9,6 +9,7 @@
 from jax.sharding import PartitionSpec as P
 
 NZ = 8
+CHUNKS = 3
 MESH = pl.DeviceIdType.MESH
 
 
@@ -81,7 +82,9 @@
     gy, z = lax.axis_index("groups"), lax.axis_index("chan")
     sx, core = lax.axis_index("space"), lax.axis_index("pair")
     main = NZ * ny
-    taps, rows, piece_rows = 27, w_all.shape[1], w_all.shape[1] // 8
+    chunk_rows = w_all.shape[1] // CHUNKS
+    piece_rows = chunk_rows // 8
+    units = CHUNKS * (n - 1)
     to_x = {"space": sx + 1 - 2 * lax.rem(sx, 2)}
     to_y = {"groups": 1 - gy}
     to_core = {"pair": 1 - core}
@@ -90,15 +93,15 @@
     has_cross = (cross_space >= 0) & (cross_space < ns)
     q = gy * 4 + lax.rem(sx, 2) * 2 + core
 
-    def flip(index, gy_flip, x_flip, core_flip):
+    def flip(gy_flip, x_flip, core_flip):
         g = 1 - gy if gy_flip else gy
         x = 1 - lax.rem(sx, 2) if x_flip else lax.rem(sx, 2)
         c = 1 - core if core_flip else core
         return g * 4 + x * 2 + c
 
-    q_x, q_y, q_d = flip(q, 0, 1, 0), flip(q, 1, 0, 0), flip(q, 1, 1, 0)
+    q_x, q_y, q_d = flip(0, 1, 0), flip(1, 0, 0), flip(1, 1, 0)
     pieces = (q, q_x, q_y, q_d)
-    partner_pieces = (flip(q, 0, 0, 1), flip(q, 0, 1, 1), flip(q, 1, 0, 1), flip(q, 1, 1, 1))
+    partner_pieces = (flip(0, 0, 1), flip(0, 1, 1), flip(1, 0, 1), flip(1, 1, 1))
 
     barrier = pltpu.get_barrier_semaphore()
     for hop in range(1, n):
@@ -125,21 +128,23 @@
     def _():
         pl.semaphore_wait(barrier, n + 2)
 
-    def w_rows(piece):
-        return pl.ds(pl.multiple_of(piece * piece_rows, piece_rows), piece_rows)
-
-    def w_copy(kind, way, step, shard, piece, target):
-        view = w_all.at[shard, w_rows(piece)]
+    def w_rows(chunk, piece):
+        first = chunk * chunk_rows + piece * piece_rows
+        return pl.ds(pl.multiple_of(first, piece_rows), piece_rows)
+
+    def w_copy(kind, way, step, chunk, shard, piece, target):
+        view = w_all.at[shard, w_rows(chunk, piece)]
         return pltpu.make_async_remote_copy(
             src_ref=view, dst_ref=view,
-            send_sem=w_send.at[kind, way, step], recv_sem=w_recv.at[kind, way, step],
+            send_sem=w_send.at[kind, way, step, chunk],
+            recv_sem=w_recv.at[kind, way, step, chunk],
             device_id=target, device_id_type=MESH,
         )
 
-    def own_z_copy(way):
+    def own_z_copy(way, chunk):
         return pltpu.make_async_remote_copy(
-            src_ref=w_ref.at[w_rows(q)], dst_ref=w_all.at[z, w_rows(q)],
-            send_sem=w_send.at[0, way, 1], recv_sem=w_recv.at[0, way, 1],
+            src_ref=w_ref.at[w_rows(chunk, q)], dst_ref=w_all.at[z, w_rows(chunk, q)],
+            send_sem=w_send.at[0, way, 1, chunk], recv_sem=w_recv.at[0, way, 1, chunk],
             device_id={"chan": z + 1 - 2 * way}, device_id_type=MESH,
         )
 
@@ -189,13 +194,13 @@
             def _():
                 act(way, step, shard_of(way, step))
 
-    for step in range(1, n):
+    for chunk in range(CHUNKS):
         for way in (0, 1):
-            @pl.when(sends_on(way, step))
+            @pl.when(sends_on(way, 1))
             def _():
-                g_copy(way, step).start()
-                if step == 1:
-                    own_z_copy(way).start()
+                own_z_copy(way, chunk).start()
+
+    acc[...] = jnp.zeros_like(acc)
 
     def start_halo(way, step, shard):
         h_copy(0, way, step, shard, True).start()
@@ -236,103 +241,141 @@
 
         lax.fori_loop(0, nx + 2, plane, 0)
 
-    def stage_a(way, step, shard):
-        w_copy(0, way, step, shard, q, to_core).wait_recv()
-        w_copy(5, way, step, shard, q, to_x).start()
-        w_copy(6, way, step, shard, q, to_y).start()
-        if step < n - 1:
-            @pl.when(sends_on(way, 1))
-            def _():
-                w_copy(0, way, step + 1, shard, q, {"chan": z + 1 - 2 * way}).start()
-        w_copy(1, way, step, shard, q, to_core).start()
+    def stage_a(way, step, chunk, shard):
+        w_copy(0, way, step, chunk, shard, q, to_core).wait_recv()
+        w_copy(5, way, step, chunk, shard, q, to_x).start()
+        w_copy(6, way, step, chunk, shard, q, to_y).start()
+
+        @pl.when((step < n - 1) & sends_on(way, 1))
+        def _():
+            w_copy(0, way, step + 1, chunk, shard, q, {"chan": z + 1 - 2 * way}).start()
+
+        w_copy(1, way, step, chunk, shard, q, to_core).start()
+
+    def stage_b(way, step, chunk, shard):
+        w_copy(5, way, step, chunk, shard, q_x, to_x).wait_recv()
+
+        @pl.when(core == 0)
+        def _():
+            w_copy(7, way, step, chunk, shard, q_x, to_y).start()
+
+        w_copy(2, way, step, chunk, shard, q_x, to_core).start()
+        w_copy(6, way, step, chunk, shard, q_y, to_y).wait_recv()
+
+        @pl.when(core == 1)
+        def _():
+            w_copy(7, way, step, chunk, shard, q_y, to_x).start()
+
+        w_copy(3, way, step, chunk, shard, q_y, to_core).start()
+
+    def stage_c(way, step, chunk, shard):
+        w_copy(7, way, step, chunk, shard, q_d, to_y).wait_recv()
+        w_copy(4, way, step, chunk, shard, q_d, to_core).start()
+
+    def multiply(shard, chunk):
+        width = cells.shape[3]
+
+        def planes(half, carry):
+            parts = []
+            for step_y in (-1, 0, 1):
+                for step_z in (-1, 0, 1):
+                    part = shifted[
+                        step_y + 1, shard, pl.ds(half * 2 + 2 - chunk, 2),
+                        pl.ds((1 - step_z) * ny, main),
+                    ]
+                    parts.append(part.reshape(2 * main, width))
+            taps = w_all[shard, pl.ds(pl.multiple_of(chunk * chunk_rows, chunk_rows), chunk_rows)]
+            product = jnp.dot(
+                jnp.concatenate(parts, axis=1), taps, preferred_element_type=jnp.float32
+            )
+            acc[pl.ds(half * 2, 2)] += product.reshape(2, main, out_ref.shape[2])
+            return carry
+
+        lax.fori_loop(0, nx // 2, planes, 0)
+
+    def compute(way, step, chunk, shard):
+        @pl.when(chunk == 0)
+        def _():
+            end_halo(way, step, shard)
+
+        for kind in range(4):
+            w_copy(
+                1 + kind, way, step, chunk, shard, partner_pieces[kind], to_core
+            ).wait_recv()
+        multiply(shard, chunk)
+
+    def run(unit, stage):
+        step, chunk = 1 + unit // CHUNKS, unit % CHUNKS
+        each_arrival(step, lambda way, step, shard: stage(way, step, chunk, shard))
+
+    def g_arrived(way, step, shard):
         g_arrival(way, step).wait_recv()
         start_halo(way, step, shard)
-
-    def stage_b(way, step, shard):
-        w_copy(5, way, step, shard, q_x, to_x).wait_recv()
-
-        @pl.when(core == 0)
-        def _():
-            w_copy(7, way, step, shard, q_x, to_y).start()
-
-        w_copy(2, way, step, shard, q_x, to_core).start()
-        w_copy(6, way, step, shard, q_y, to_y).wait_recv()
-
-        @pl.when(core == 1)
-        def _():
-            w_copy(7, way, step, shard, q_y, to_x).start()
-
-        w_copy(3, way, step, shard, q_y, to_core).start()
-
-    def stage_c(way, step, shard):
-        w_copy(7, way, step, shard, q_d, to_y).wait_recv()
-        w_copy(4, way, step, shard, q_d, to_core).start()
-
-    def multiply(shard, first):
-        width = cells.shape[3]
-        weights = w_all.at[shard]
-
-        def planes(half, carry):
-            parts = []
-            for step_x in (-1, 0, 1):
-                for step_y in (-1, 0, 1):
-                    for step_z in (-1, 0, 1):
-                        part = shifted[
-                            step_y + 1, shard, pl.ds(half * 2 + 1 - step_x, 2),
-                            pl.ds((1 - step_z) * ny, main),
-                        ]
-                        parts.append(part.reshape(2 * main, width))
-            product = jnp.dot(
-                jnp.concatenate(parts, axis=1), weights[...],
-                preferred_element_type=jnp.float32,
-            ).reshape(2, main, out_ref.shape[2])
-            if first:
-                acc[pl.ds(half * 2, 2)] = product
-            else:
-                acc[pl.ds(half * 2, 2)] += product
-            return carry
-
-        lax.fori_loop(0, nx // 2, planes, 0)
-
-    def compute(way, step, shard):
-        end_halo(way, step, shard)
-        for kind in range(4):
-            w_copy(1 + kind, way, step, shard, partner_pieces[kind], to_core).wait_recv()
-        multiply(shard, False)
 
     own_g.wait()
     start_halo(0, 0, z)
     own_w.wait()
     end_halo(0, 0, z)
-    each_arrival(1, stage_a)
-    multiply(z, True)
-    for step in range(1, n):
-        each_arrival(step, stage_b)
-        if step + 1 < n:
-            each_arrival(step + 1, stage_a)
-        each_arrival(step, stage_c)
-        each_arrival(step, compute)
+
+    def turn(k, carry):
+        @pl.when(k < units)
+        def _():
+            run(k, stage_a)
+
+        @pl.when((k % 2 == 0) & (k // 2 + 1 < n))
+        def _():
+            step = k // 2 + 1
+            for way in (0, 1):
+                @pl.when(sends_on(way, step))
+                def _():
+                    g_copy(way, step).start()
+
+        @pl.when((k >= 1) & (k < units + 1))
+        def _():
+            run(k - 1, stage_b)
+
+        @pl.when((k >= 2) & (k < units + 2))
+        def _():
+            run(k - 2, stage_c)
+
+        @pl.when((k < units) & (k % CHUNKS == CHUNKS - 1))
+        def _():
+            each_arrival(1 + k // CHUNKS, g_arrived)
+
+        @pl.when(k < CHUNKS)
+        def _():
+            multiply(z, k)
+
+        @pl.when(k >= 3)
+        def _():
+            run(k - 3, compute)
+
+        return carry
+
+    lax.fori_loop(0, units + 3, turn, 0)
     out_ref[...] = acc[...].astype(out_ref.dtype)
 
-    def end_sends(way, step, shard):
-        w_copy(5, way, step, shard, q, to_x).wait_send()
-        w_copy(6, way, step, shard, q, to_y).wait_send()
+    def end_sends(way, step, chunk, shard):
+        w_copy(5, way, step, chunk, shard, q, to_x).wait_send()
+        w_copy(6, way, step, chunk, shard, q, to_y).wait_send()
         for kind in range(4):
-            w_copy(1 + kind, way, step, shard, pieces[kind], to_core).wait_send()
+            w_copy(1 + kind, way, step, chunk, shard, pieces[kind], to_core).wait_send()
 
         @pl.when(core == 0)
         def _():
-            w_copy(7, way, step, shard, q_x, to_y).wait_send()
+            w_copy(7, way, step, chunk, shard, q_x, to_y).wait_send()
 
         @pl.when(core == 1)
         def _():
-            w_copy(7, way, step, shard, q_y, to_x).wait_send()
-
-        if step < n - 1:
-            @pl.when(sends_on(way, 1))
-            def _():
-                w_copy(0, way, step + 1, shard, q, {"chan": z + 1 - 2 * way}).wait_send()
-        end_halo_sends(way, step, shard)
+            w_copy(7, way, step, chunk, shard, q_y, to_x).wait_send()
+
+        @pl.when((step < n - 1) & sends_on(way, 1))
+        def _():
+            w_copy(0, way, step + 1, chunk, shard, q, {"chan": z + 1 - 2 * way}).wait_send()
+
+        @pl.when(chunk == 0)
+        def _():
+            end_halo_sends(way, step, shard)
 
     def end_halo_sends(way, step, shard):
         h_copy(0, way, step, shard, True).wait_send()
@@ -342,14 +385,21 @@
             h_copy(1, way, step, shard, True).wait_send()
 
     end_halo_sends(0, 0, z)
-    for step in range(1, n):
-        each_arrival(step, end_sends)
-        for way in (0, 1):
+
+    def close(unit, carry):
+        run(unit, end_sends)
+        return carry
+
+    lax.fori_loop(0, units, close, 0)
+    for way in (0, 1):
+        @pl.when(sends_on(way, 1))
+        def _():
+            for chunk in range(CHUNKS):
+                own_z_copy(way, chunk).wait_send()
+        for step in range(1, n):
             @pl.when(sends_on(way, step))
             def _():
                 g_copy(way, step).wait_send()
-                if step == 1:
-                    own_z_copy(way).wait_send()
 
 
 def body_gather(n, ns, grad_out, conv_weight, pre_act, down_weight):
@@ -378,7 +428,7 @@
             vmem((n, nx + 2, main + 2 * NZ, channels), jnp.bfloat16),
             vmem((3, n, nx + 2, main + 2 * ny, channels), jnp.bfloat16),
             vmem((nx, main, wide), jnp.float32),
-            dma((8, 2, n)), dma((8, 2, n)),
+            dma((8, 2, n, CHUNKS)), dma((8, 2, n, CHUNKS)),
             dma((2, n)), dma((2, n)),
             dma((2, 2, n)), dma((2, 2, n)),
             dma((2,)),

time: 101 us -> 92.9 us (0.920); the launches traced: 99 us -> 92.8 us
  Pallas kernels: 85.7 us -> 79.4 us
    pallas_call x1, Pallas kernels: 85.7 us -> 79.4 us  [body_gather(): pl.pallas_call(functools.partial(conv_kernel, n, ns, nx, ny), out_shape=j...]
where the time goes in v2:
time: 92.9 us; the launch traced here: 92.8 us
  Pallas kernels  79.4 us (85%)
  local copies, waits for them, and re-layouts  6.98 us (8%)
  matrix products  3.64 us (4%)
  other arithmetic  2.66 us (3%)
    pallas_call x1, Pallas kernels, body_gather(): pl.pallas_call(functools.partial(conv_kernel, n, ns, nx, ny), out_shape=j...  79.4 us
    convert_element_type x1, local copies, waits for them, and re-layouts, finish(): return result.astype(jnp.bfloat16)  4.47 us
    dot_general x1, matrix products, finish(): lax.dot_general(grad_pre, down_weight, (((2,), (2,)), ((), ())), preferre...  3.64 us
    unnamed x5, local copies, waits for them, and re-layouts  2.08 us

profile of v2, /device:TPU:0, one launch (start us, length us, event | category | flops | bytes accessed | tf_op | source)
XLA Modules:
  0.0 92.8 jit_solution(13919273733620649210)
XLA Ops:
  0.0 0.0 copy-start
  0.0 2.1 %copy.8 = bf16[128,4,1024]{0,2,1:T(8,128)(2,1)S(1)} copy(bf16[128,4,1024]{2,1,0:T(4,128)(2,1)} %param.4) | data formatting | bytes 2097152 | tf_op args[0]
  2.1 0.2 copy.10
  2.3 0.2 copy_bitcast_fusion
  2.5 1.1 %pad_maximum_fusion.s_ref = bf16[4,4,272,128]{3,2,1,0:T(8,128)(2,1)} fusion(bf16[4,4,8,128]{3,2,1,0:T(8,128)(2,1)S(1)} %get-tuple-element.6, bf16[4,4,8,128]{3,2,1,0:T(8,128)(2,1)S(1)} %get-tuple-element.5, bf16[4,4,256,128]{3,2,1,0:T(8,128)(2,1)S(1)} %bitcast.35), kind=kLoop, calls=%fused_computation.15 | loop fusion | flops 3342336 | bytes 2228224 | tf_op jit(solution)/shard_map/concatenate | solution.py:417
  3.6 79.4 %shard_map.46 = bf16[4,256,512]{2,1,0:T(8,128)(2,1)} custom-call(bf16[4,4,272,128]{3,2,1,0:T(8,128)(2,1)} %pad_maximum_fusion.s_ref, bf16[3456,512]{1,0:T(8,128)(2,1)} %bitcast.37), custom_call_target="tpu_custom_call" | custom-call | flops 14495514624 | bytes 8388608 | tf_op jit(solution)/shard_map/pallas_call | solution.py:421
  83.0 0.0 copy-start.1
  83.0 1.6 %convert_bitcast_fusion = f32[4,32,8,512]{3,1,2,0:T(8,128)S(1)} fusion(bf16[4,8,32,512]{3,2,1,0:T(8,128)(2,1)} %bitcast.36), kind=kLoop, calls=%fused_computation.12 | loop fusion | flops 524288 | bytes 3145728 | tf_op jit(solution)/shard_map/convert_element_type | solution.py:58
  84.6 0.0 copy-done
  84.6 0.0 copy-done.1
  84.6 3.6 %convolution_convert_fusion = bf16[4,256,8,256]{3,1,2,0:T(8,128)(2,1)S(1)} fusion(bf16[8,256,512]{2,1,0:T(8,128)(2,1)S(1)} %copy-done, bf16[4,256,512]{2,1,0:T(8,128)(2,1)S(1)} %copy-done.1, f32[4,32,8,512]{3,1,2,0:T(8,128)S(1)} %convert_bitcast_fusion), kind=kOutput, calls=%fused_computation.4 | convolution fusion | flops 2155347968 | bytes 9437184 | tf_op jit(solution)/shard_map/dot_general | solution.py:59
  88.3 4.5 %copy.12 = bf16[4,256,8,256]{3,2,1,0:T(8,128)(2,1)} copy(bf16[4,256,8,256]{3,1,2,0:T(8,128)(2,1)S(1)} %convolution_convert_fusion) | data formatting | bytes 8388608 | tf_op jit(solution)/shard_map/convert_element_type | solution.py:62
  (1 shorter events, 0.0 us)
Async XLA Ops:
  0.0 84.6 %copy-start = (bf16[8,256,512]{2,1,0:T(8,128)(2,1)S(1)}, bf16[8,256,512]{2,1,0:T(8,128)(2,1)}, u32[]{:S(2)}) copy-start(bf16[8,256,512]{2,1,0:T(8,128)(2,1)} %param.7) | copy-start | bytes 6291460
  83.0 1.6 %copy-start.1 = (bf16[4,256,512]{2,1,0:T(8,128)(2,1)S(1)}, bf16[4,256,512]{2,1,0:T(8,128)(2,1)}, u32[]{:S(2)}) copy-start(bf16[4,256,512]{2,1,0:T(8,128)(2,1)} %param.6) | copy-start | bytes 3145732

commit v3 on v2

--- a/solution.py
+++ b/solution.py
@@ -241,15 +241,19 @@
 
         lax.fori_loop(0, nx + 2, plane, 0)
 
+    def stage_z(way, step, chunk, shard):
+        @pl.when(sends_on(way, 1))
+        def _():
+            w_copy(0, way, step, chunk, shard, q, to_core).wait_recv()
+            w_copy(0, way, step + 1, chunk, shard, q, {"chan": z + 1 - 2 * way}).start()
+
     def stage_a(way, step, chunk, shard):
-        w_copy(0, way, step, chunk, shard, q, to_core).wait_recv()
+        @pl.when(jnp.logical_not(sends_on(way, 1)))
+        def _():
+            w_copy(0, way, step, chunk, shard, q, to_core).wait_recv()
+
         w_copy(5, way, step, chunk, shard, q, to_x).start()
         w_copy(6, way, step, chunk, shard, q, to_y).start()
-
-        @pl.when((step < n - 1) & sends_on(way, 1))
-        def _():
-            w_copy(0, way, step + 1, chunk, shard, q, {"chan": z + 1 - 2 * way}).start()
-
         w_copy(1, way, step, chunk, shard, q, to_core).start()
 
     def stage_b(way, step, chunk, shard):
@@ -318,13 +322,21 @@
     end_halo(0, 0, z)
 
     def turn(k, carry):
+        @pl.when((k >= 1) & (2 * k - 1 < units))
+        def _():
+            run(2 * k - 1, stage_z)
+
+        @pl.when(2 * k < units)
+        def _():
+            run(2 * k, stage_z)
+
         @pl.when(k < units)
         def _():
             run(k, stage_a)
 
-        @pl.when((k % 2 == 0) & (k // 2 + 1 < n))
-        def _():
-            step = k // 2 + 1
+        @pl.when(k + 1 < n)
+        def _():
+            step = k + 1
             for way in (0, 1):
                 @pl.when(sends_on(way, step))
                 def _():
@@ -369,7 +381,7 @@
         def _():
             w_copy(7, way, step, chunk, shard, q_y, to_x).wait_send()
 
-        @pl.when((step < n - 1) & sends_on(way, 1))
+        @pl.when(sends_on(way, 1))
         def _():
             w_copy(0, way, step + 1, chunk, shard, q, {"chan": z + 1 - 2 * way}).wait_send()
 

time: 92.9 us -> 93.1 us (level)
  no operation moved by 1% of the time
where the time goes in v3:
time: 93.1 us; the launch traced here: 92.9 us
  Pallas kernels  79.5 us (85%)
  local copies, waits for them, and re-layouts  6.98 us (7%)
  matrix products  3.64 us (4%)
  other arithmetic  2.66 us (3%)
    pallas_call x1, Pallas kernels, body_gather(): pl.pallas_call(functools.partial(conv_kernel, n, ns, nx, ny), out_shape=j...  79.5 us
    convert_element_type x1, local copies, waits for them, and re-layouts, finish(): return result.astype(jnp.bfloat16)  4.47 us
    dot_general x1, matrix products, finish(): lax.dot_general(grad_pre, down_weight, (((2,), (2,)), ((), ())), preferre...  3.64 us
    unnamed x5, local copies, waits for them, and re-layouts  2.08 us

profile of v3, /device:TPU:0, one launch (start us, length us, event | category | flops | bytes accessed | tf_op | source)
XLA Modules:
  0.0 92.9 jit_solution(15355633712790714105)
XLA Ops:
  0.0 0.0 copy-start
  0.0 2.1 %copy.8 = bf16[128,4,1024]{0,2,1:T(8,128)(2,1)S(1)} copy(bf16[128,4,1024]{2,1,0:T(4,128)(2,1)} %param.4) | data formatting | bytes 2097152 | tf_op args[0]
  2.1 0.2 copy.10
  2.3 0.2 copy_bitcast_fusion
  2.5 1.1 %pad_maximum_fusion.s_ref = bf16[4,4,272,128]{3,2,1,0:T(8,128)(2,1)} fusion(bf16[4,4,8,128]{3,2,1,0:T(8,128)(2,1)S(1)} %get-tuple-element.6, bf16[4,4,8,128]{3,2,1,0:T(8,128)(2,1)S(1)} %get-tuple-element.5, bf16[4,4,256,128]{3,2,1,0:T(8,128)(2,1)S(1)} %bitcast.35), kind=kLoop, calls=%fused_computation.15 | loop fusion | flops 3342336 | bytes 2228224 | tf_op jit(solution)/shard_map/concatenate | solution.py:429
  3.6 79.5 %shard_map.46 = bf16[4,256,512]{2,1,0:T(8,128)(2,1)} custom-call(bf16[4,4,272,128]{3,2,1,0:T(8,128)(2,1)} %pad_maximum_fusion.s_ref, bf16[3456,512]{1,0:T(8,128)(2,1)} %bitcast.37), custom_call_target="tpu_custom_call" | custom-call | flops 14495514624 | bytes 8388608 | tf_op jit(solution)/shard_map/pallas_call | solution.py:433
  83.1 0.0 copy-start.1
  83.2 1.6 %convert_bitcast_fusion = f32[4,32,8,512]{3,1,2,0:T(8,128)S(1)} fusion(bf16[4,8,32,512]{3,2,1,0:T(8,128)(2,1)} %bitcast.36), kind=kLoop, calls=%fused_computation.12 | loop fusion | flops 524288 | bytes 3145728 | tf_op jit(solution)/shard_map/convert_element_type | solution.py:58
  84.7 0.0 copy-done
  84.7 0.0 copy-done.1
  84.8 3.6 %convolution_convert_fusion = bf16[4,256,8,256]{3,1,2,0:T(8,128)(2,1)S(1)} fusion(bf16[8,256,512]{2,1,0:T(8,128)(2,1)S(1)} %copy-done, bf16[4,256,512]{2,1,0:T(8,128)(2,1)S(1)} %copy-done.1, f32[4,32,8,512]{3,1,2,0:T(8,128)S(1)} %convert_bitcast_fusion), kind=kOutput, calls=%fused_computation.4 | convolution fusion | flops 2155347968 | bytes 9437184 | tf_op jit(solution)/shard_map/dot_general | solution.py:59
  88.4 4.5 %copy.12 = bf16[4,256,8,256]{3,2,1,0:T(8,128)(2,1)} copy(bf16[4,256,8,256]{3,1,2,0:T(8,128)(2,1)S(1)} %convolution_convert_fusion) | data formatting | bytes 8388608 | tf_op jit(solution)/shard_map/convert_element_type | solution.py:62
  (1 shorter events, 0.0 us)
Async XLA Ops:
  0.0 84.7 %copy-start = (bf16[8,256,512]{2,1,0:T(8,128)(2,1)S(1)}, bf16[8,256,512]{2,1,0:T(8,128)(2,1)}, u32[]{:S(2)}) copy-start(bf16[8,256,512]{2,1,0:T(8,128)(2,1)} %param.7) | copy-start | bytes 6291460
  83.1 1.6 %copy-start.1 = (bf16[4,256,512]{2,1,0:T(8,128)(2,1)S(1)}, bf16[4,256,512]{2,1,0:T(8,128)(2,1)}, u32[]{:S(2)}) copy-start(bf16[4,256,512]{2,1,0:T(8,128)(2,1)} %param.6) | copy-start | bytes 3145732

commit v4 on v2

--- a/solution.py
+++ b/solution.py
@@ -60,6 +60,39 @@
         grad_pre, down_weight, (((2,), (2,)), ((), ())), preferred_element_type=jnp.float32
     )
     return result.astype(jnp.bfloat16)
+
+
+def down_kernel(taps, grad_ref, weight_ref, out_ref, total):
+    rows = grad_ref.shape[1]
+    for tap in range(taps):
+        part = lax.dot_general(
+            grad_ref[0], weight_ref[tap], (((1,), (1,)), ((), ())),
+            preferred_element_type=jnp.float32,
+        )
+        for lanes in range(0, part.shape[1], 128):
+            total[lanes // 128, pl.ds(tap, rows, stride=taps), :] = part[:, lanes : lanes + 128]
+    for half in range(total.shape[0]):
+        out_ref[0, :, half * 128 : half * 128 + 128] = total[half].astype(out_ref.dtype)
+
+
+def finish_planes(grad_act, pre_act, down_weight):
+    values = pre_act.astype(jnp.float32)
+    grad_pre = (grad_act.astype(jnp.float32) * gelu_slope(values)).astype(jnp.bfloat16)
+    nx, rows, channels = grad_pre.shape
+    taps, fine, _ = down_weight.shape
+    result = pl.pallas_call(
+        functools.partial(down_kernel, taps),
+        grid=(nx,),
+        out_shape=jax.ShapeDtypeStruct((nx, rows * taps, fine), jnp.bfloat16),
+        in_specs=[
+            pl.BlockSpec((1, rows, channels), lambda i: (i, 0, 0)),
+            pl.BlockSpec((taps, fine, channels), lambda i: (0, 0, 0)),
+        ],
+        out_specs=pl.BlockSpec((1, rows * taps, fine), lambda i: (i, 0, 0)),
+        scratch_shapes=[pltpu.VMEM((fine // 128, rows * taps, 128), jnp.float32)],
+        compiler_params=pltpu.CompilerParams(vmem_limit_bytes=32 * 2**20),
+    )(grad_pre, down_weight)
+    return result.reshape(nx, rows, taps, fine)
 
 
 def body_blocks(grad_out, conv_weight, pre_act, down_weight):
@@ -442,7 +475,7 @@
         ),
     )(send, weights)
     grad_act = grad_act.reshape(nx, NZ, ny, wide).transpose(0, 2, 1, 3).reshape(nx, main, wide)
-    return finish(grad_act, pre_act, down_weight)
+    return finish_planes(grad_act, pre_act, down_weight)
 
 
 def solution(mesh):

time: 92.9 us -> 90.9 us (0.978)
  Pallas kernels: 79.4 us -> 84.1 us
  local copies, waits for them, and re-layouts: 6.98 us -> 2.48 us
  matrix products: 3.64 us -> 0 us
  other arithmetic: 2.66 us -> 4.12 us
    pallas_call x0 -> x1, Pallas kernels: none -> 4.66 us  [finish_planes(): pl.pallas_call(functools.partial(down_kernel, taps), grid=(nx,), out_shap...]
    convert_element_type x1 -> x0, local copies, waits for them, and re-layouts: 4.47 us -> none  [finish(): return result.astype(jnp.bfloat16)]
    dot_general x1 -> x0, matrix products: 3.64 us -> none  [finish(): lax.dot_general(grad_pre, down_weight, (((2,), (2,)), ((), ())), preferre...]
    convert_element_type x1 -> x2, other arithmetic: 1.58 us -> 3.03 us  [the longest x1 1.58 us: finish_planes(): grad_act.astype(jnp.float32) * gelu_slope(values)]
where the time goes in v4:
time: 90.9 us; the launch traced here: 90.7 us
  Pallas kernels  84.1 us (93%)
  other arithmetic  4.12 us (5%)
  local copies, waits for them, and re-layouts  2.48 us (3%)
    pallas_call x1, Pallas kernels, body_gather(): pl.pallas_call(functools.partial(conv_kernel, n, ns, nx, ny), out_shape=j...  79.4 us
    pallas_call x1, Pallas kernels, finish_planes(): pl.pallas_call(functools.partial(down_kernel, taps), grid=(nx,), out_shap...  4.66 us
    unnamed x5, local copies, waits for them, and re-layouts  2.05 us

profile of v4, /device:TPU:0, one launch (start us, length us, event | category | flops | bytes accessed | tf_op | source)
XLA Modules:
  0.0 90.7 jit_solution(15339643255839134495)
XLA Ops:
  0.0 1.9 %copy.7 = bf16[128,4,1024]{0,2,1:T(8,128)(2,1)S(1)} copy(bf16[128,4,1024]{2,1,0:T(4,128)(2,1)} %param.4) | data formatting | bytes 2097152 | tf_op args[0]
  1.9 0.2 copy.9
  2.2 0.2 copy_bitcast_fusion
  2.4 1.1 %pad_maximum_fusion.s_ref = bf16[4,4,272,128]{3,2,1,0:T(8,128)(2,1)} fusion(bf16[4,4,8,128]{3,2,1,0:T(8,128)(2,1)S(1)} %get-tuple-element.6, bf16[4,4,8,128]{3,2,1,0:T(8,128)(2,1)S(1)} %get-tuple-element.5, bf16[4,4,256,128]{3,2,1,0:T(8,128)(2,1)S(1)} %bitcast.25), kind=kLoop, calls=%fused_computation.12 | loop fusion | flops 3342336 | bytes 2228224 | tf_op jit(solution)/shard_map/concatenate | solution.py:450
  3.5 79.4 %shard_map.46 = bf16[4,256,512]{2,1,0:T(8,128)(2,1)} custom-call(bf16[4,4,272,128]{3,2,1,0:T(8,128)(2,1)} %pad_maximum_fusion.s_ref, bf16[3456,512]{1,0:T(8,128)(2,1)} %bitcast.27), custom_call_target="tpu_custom_call" | custom-call | flops 14495514624 | bytes 8388608 | tf_op jit(solution)/shard_map/pallas_call | solution.py:454
  82.9 0.0 copy-start.1
  82.9 1.6 %convert.3 = f32[4,8,32,512]{3,2,1,0:T(8,128)S(1)} convert(bf16[4,8,32,512]{3,2,1,0:T(8,128)(2,1)} %bitcast.26) | non-fusion elementwise | flops 524288 | bytes 3145728 | tf_op jit(solution)/shard_map/convert_element_type | solution.py:80
  84.5 0.0 copy-done.1
  84.5 0.0 copy-start
  84.5 1.5 %fusion.7.grad_ref = bf16[4,256,512]{2,1,0:T(8,128)(2,1)S(1)} fusion(bf16[4,256,512]{2,1,0:T(8,128)(2,1)S(1)} %copy-done.1, f32[4,8,32,512]{3,2,1,0:T(8,128)S(1)} %convert.3), kind=kLoop, calls=%fused_computation.11 | loop fusion | flops 5767168 | bytes 4194304 | tf_op jit(solution)/shard_map/convert_element_type | solution.py:80
  85.9 0.1 copy-done
  86.1 4.7 %shard_map.47 = bf16[4,2048,256]{2,1,0:T(8,128)(2,1)} custom-call(bf16[4,256,512]{2,1,0:T(8,128)(2,1)S(1)} %fusion.7.grad_ref, bf16[8,256,512]{2,1,0:T(8,128)(2,1)S(1)} %copy-done), custom_call_target="tpu_custom_call" | custom-call | tf_op jit(solution)/shard_map/pallas_call | solution.py:83
  (1 shorter events, 0.0 us)
Async XLA Ops:
  82.9 1.6 %copy-start.1 = (bf16[4,256,512]{2,1,0:T(8,128)(2,1)S(1)}, bf16[4,256,512]{2,1,0:T(8,128)(2,1)}, u32[]{:S(2)}) copy-start(bf16[4,256,512]{2,1,0:T(8,128)(2,1)} %param.6) | copy-start | bytes 3145732
  84.5 1.6 %copy-start = (bf16[8,256,512]{2,1,0:T(8,128)(2,1)S(1)}, bf16[8,256,512]{2,1,0:T(8,128)(2,1)}, u32[]{:S(2)}) copy-start(bf16[8,256,512]{2,1,0:T(8,128)(2,1)} %weight_ref.1) | copy-start | bytes 6291460
